TPU v7x, 512 devices: a whole 4x4x16 slice. The times are simulated.
512 devices in a mesh: section: 16 (over x, y), row: 4 (over z_hi, core), col: 8 (over z_lo).
Axes of the slice: x: 4, y: 4, z: 16 (z_hi: 2, z_lo: 8; z = z_hi * 8 + z_lo), core: 2. Of those that a mesh axis runs over, the one named last changes fastest.
Arguments:
- inputs: bfloat16 [16, 3, 128, 2048], P('section', None, 'row', 'col'), may hold values from -6 to 6
- sample_ids: int32 [18], replicated, may hold values from 0 to 15
- send_base: bfloat16 [16, 16, 128, 2048], P('section', None, 'row', 'col'), may hold values from -1.796875 to 1.796875
- recv_base: bfloat16 [16, 16, 128, 2048], P('section', None, 'row', 'col'), may hold values from -1.796875 to 1.796875
- w_up: bfloat16 [16, 2048, 8192], P('section', 'col', 'row'), may hold values from -0.125 to 0.125
- w_down: bfloat16 [16, 8192, 2048], P('section', 'row', 'col'), may hold values from -0.0625 to 0.0625
- cotangent: bfloat16 [16, 3, 128, 2048], P('section', None, 'row', 'col'), may hold values from -6 to 6
Outputs:
- section_input: bfloat16 [16, 3, 128, 2048], P('section', None, 'row', 'col')
- section_output: bfloat16 [16, 3, 128, 2048], P('section', None, 'row', 'col')
- input_grad: bfloat16 [16, 3, 128, 2048], P('section', None, 'row', 'col')
- grad_up: bfloat16 [16, 2048, 8192], P('section', 'col', 'row')
- grad_down: bfloat16 [16, 8192, 2048], P('section', 'row', 'col')
All inputs are finite; a program needn't handle non-finite values.
Results may differ from a plain program's by a relative error of at most 0.04.
Values may be sent and summed in bfloat16 or wider, within the bound.
A program may use at most 64 MiB of HBM per device.

v0:
```python
import jax
import jax.numpy as jnp
from jax import lax
from jax.sharding import PartitionSpec as P


def from_behind(block, axis, distance):
    devices = range(lax.axis_size(axis))
    route = [(i - distance, i) for i in devices if i - distance in devices]
    return lax.ppermute(block, axis, route)


def silu_slope(value):
    sig = jax.nn.sigmoid(value)
    return sig * (1.0 + value * (1.0 - sig))


def pick(table, index):
    return lax.dynamic_index_in_dim(table, index, 0, keepdims=False)


def per_device(inputs, sample_ids, send_base, recv_base, w_up, w_down, cotangent):
    section = lax.axis_index("section")
    sections = lax.axis_size("section")
    ticks = inputs.shape[1]
    piece_rows = inputs.shape[2]
    up_block = w_up[0]
    down_block = w_down[0]
    contract_last = (((1,), (1,)), ((), ()))
    contract_first = (((0,), (0,)), ((), ()))
    gathered_in = []
    hidden_pre = []
    hidden_act = []
    seen_in = []
    seen_out = []
    sending = None
    for tick in range(ticks):
        sample = pick(sample_ids, tick - section + sections - 1)
        if tick == 0:
            act_in = inputs[0, tick]
        else:
            arrived = from_behind(sending, "section", 1)
            rebuilt = (
                pick(recv_base[0], sample).astype(jnp.float32) + arrived.astype(jnp.float32)
            ).astype(jnp.bfloat16)
            act_in = jnp.where(section == 0, inputs[0, tick], rebuilt)
        full_in = lax.all_gather(act_in, "row", axis=0, tiled=True)
        partial_value = jnp.dot(full_in, up_block, preferred_element_type=jnp.float32)
        pre_keep = lax.psum(partial_value.astype(jnp.bfloat16), "col").astype(jnp.float32)
        act_full = jax.nn.silu(pre_keep).astype(jnp.bfloat16)

        def down_term(start, count, act_full=act_full):
            return jnp.dot(act_full, down_block, preferred_element_type=jnp.float32)

        mixed = lax.psum_scatter(
            down_term(jnp.int32(0), piece_rows * lax.axis_size("row")).astype(jnp.bfloat16),
            "row",
            scatter_dimension=0,
            tiled=True,
        ).astype(jnp.float32)
        act_out = (act_in.astype(jnp.float32) + mixed).astype(jnp.bfloat16)
        stored = pick(send_base[0], sample)
        sending = (act_out.astype(jnp.float32) - stored.astype(jnp.float32)).astype(jnp.bfloat16)
        gathered_in.append(full_in)
        hidden_pre.append(pre_keep)
        hidden_act.append(act_full)
        seen_in.append(act_in)
        seen_out.append(act_out)
    grads_full = [None] * ticks
    pre_grads = [None] * ticks
    seen_grad = [None] * ticks
    sending = None
    for turn in range(ticks):
        tick = ticks - 1 - turn
        if turn == 0:
            grad_out = cotangent[0, tick]
        else:
            arrived = from_behind(sending, "section", -1)
            grad_out = jnp.where(section == sections - 1, cotangent[0, tick], arrived)
        full_grad = lax.all_gather(grad_out, "row", axis=0, tiled=True)
        partial_value = lax.dot_general(
            full_grad, down_block, contract_last, preferred_element_type=jnp.float32
        )
        pre_keep = hidden_pre[tick]
        grad_act = lax.psum(partial_value.astype(jnp.bfloat16), "col").astype(jnp.float32)
        grad_pre = (grad_act * silu_slope(pre_keep)).astype(jnp.bfloat16)

        def feature_term(start, count, grad_pre=grad_pre):
            return lax.dot_general(
                grad_pre, up_block, contract_last, preferred_element_type=jnp.float32
            )

        returned = lax.psum_scatter(
            feature_term(jnp.int32(0), piece_rows * lax.axis_size("row")).astype(jnp.bfloat16),
            "row",
            scatter_dimension=0,
            tiled=True,
        ).astype(jnp.float32)
        grad_in = (grad_out.astype(jnp.float32) + returned).astype(jnp.bfloat16)
        sending = grad_in
        grads_full[tick] = full_grad
        pre_grads[tick] = grad_pre
        seen_grad[tick] = grad_in
    flat_in = jnp.concatenate(gathered_in, axis=0)
    flat_act = jnp.concatenate(hidden_act, axis=0)
    flat_grad = jnp.concatenate(grads_full, axis=0)
    flat_pre = jnp.concatenate(pre_grads, axis=0)
    grad_up = lax.dot_general(flat_in, flat_pre, contract_first, preferred_element_type=jnp.float32)
    grad_down = lax.dot_general(
        flat_act, flat_grad, contract_first, preferred_element_type=jnp.float32
    )
    return (
        jnp.stack(seen_in)[None],
        jnp.stack(seen_out)[None],
        jnp.stack(seen_grad)[None],
        grad_up.astype(jnp.bfloat16)[None],
        grad_down.astype(jnp.bfloat16)[None],
    )


def solution(mesh):
    placed = (
        P("section", None, "row", "col"),
        P(),
        P("section", None, "row", "col"),
        P("section", None, "row", "col"),
        P("section", "col", "row"),
        P("section", "row", "col"),
        P("section", None, "row", "col"),
    )
    return jax.shard_map(
        per_device,
        mesh=mesh,
        in_specs=placed,
        out_specs=(
            P("section", None, "row", "col"),
            P("section", None, "row", "col"),
            P("section", None, "row", "col"),
            P("section", "col", "row"),
            P("section", "row", "col"),
        ),
        check_vma=False,
    )
```

profile of v0, /device:TPU:1, one launch (start us, length us, event | category | flops | bytes accessed | tf_op | source)
XLA Modules:
  0.0 986.5 jit_solution(16953147231518005086)
XLA Ops:
  7.2 1.4 slice_bitcast_fusion
  8.6 20.6 %all-gather = bf16[1,1,128,256]{3,2,1,0:T(8,128)(2,1)S(1)} all-gather(bf16[1,1,32,256]{3,2,1,0:T(8,128)(2,1)S(1)} %get-tuple-element.12), channel_id=2, replica_groups=mesh['section'=16,'row'=4,'col'=8] {'row'}, dimensions={2}, use_global_device_ids=true | all-gather | bytes 81920 | tf_op jit(solution)/shard_map/all_gather | solution.py:47
  29.3 2.3 convolution_convert_fusion.7
  31.7 116.6 %all-reduce.7.cloned.1.call-done = bf16[128,2048]{1,0:T(8,128)(2,1)} async-done(((bf16[128,2048]{1,0:T(8,128)(2,1)}), bf16[128,2048]{1,0:T(8,128)(2,1)}) %all-reduce.7.cloned.1.call-update) | async-done | bytes 524304 | tf_op jit(solution)/shard_map/psum | solution.py:49
  153.3 48.2 %reduce-scatter.7.cloned.1.call-done = bf16[32,256]{1,0:T(8,128)(2,1)} async-done(((bf16[128,256]{1,0:T(8,128)(2,1)}), bf16[32,256]{1,0:T(8,128)(2,1)}) %reduce-scatter.7.cloned.1.call-update) | async-done | bytes 16400 | tf_op jit(solution)/shard_map/reduce_scatter | solution.py:55
  201.5 1.3 fusion.69
  202.8 3.3 collective-permute-start
  208.8 14.6 %all_gather.19 = bf16[128,256]{1,0:T(8,128)(2,1)S(1)} all-gather(bf16[32,256]{1,0:T(8,128)(2,1)S(1)} %fusion.66), channel_id=1, replica_groups=mesh['section'=16,'row'=4,'col'=8] {'row'}, dimensions={0}, use_global_device_ids=true | all-gather | bytes 81920 | tf_op jit(solution)/shard_map/all_gather | solution.py:47
  224.6 109.4 %all-reduce.9.cloned.1.call-done = bf16[128,2048]{1,0:T(8,128)(2,1)} async-done(((bf16[128,2048]{1,0:T(8,128)(2,1)}), bf16[128,2048]{1,0:T(8,128)(2,1)}) %all-reduce.9.cloned.1.call-update) | async-done | bytes 524304 | tf_op jit(solution)/shard_map/psum | solution.py:49
  337.2 19.8 %all-gather.1 = bf16[1,1,128,256]{3,2,1,0:T(8,128)(2,1)S(1)} all-gather(bf16[1,1,32,256]{3,2,1,0:T(8,128)(2,1)S(1)} %slice-done), channel_id=3, replica_groups=mesh['section'=16,'row'=4,'col'=8] {'row'}, dimensions={2}, use_global_device_ids=true | all-gather | bytes 81920 | tf_op jit(solution)/shard_map/all_gather | solution.py:80
  357.0 30.1 %reduce-scatter.9.cloned.1.call-done = bf16[32,256]{1,0:T(8,128)(2,1)} async-done(((bf16[128,256]{1,0:T(8,128)(2,1)}), bf16[32,256]{1,0:T(8,128)(2,1)}) %reduce-scatter.9.cloned.1.call-update) | async-done | bytes 16400 | tf_op jit(solution)/shard_map/reduce_scatter | solution.py:55
  388.4 3.3 collective-permute-start.1
  395.6 14.6 %all_gather.20 = bf16[128,256]{1,0:T(8,128)(2,1)S(1)} all-gather(bf16[32,256]{1,0:T(8,128)(2,1)S(1)} %fusion.67), channel_id=1, replica_groups=mesh['section'=16,'row'=4,'col'=8] {'row'}, dimensions={0}, use_global_device_ids=true | all-gather | bytes 81920 | tf_op jit(solution)/shard_map/all_gather | solution.py:47
  411.5 113.9 %all-reduce.15.cloned.1.call-done = (bf16[128,2048]{1,0:T(8,128)(2,1)}, bf16[128,2048]{1,0:T(8,128)(2,1)}) async-done(((bf16[128,2048]{1,0:T(8,128)(2,1)}, bf16[128,2048]{1,0:T(8,128)(2,1)}), (bf16[128,2048]{1,0:T(8,128)(2,1)}, bf16[128,2048]{1,0:T(8,128)(2,1)})) %all-reduce.15.cloned.1.call-update) | async-done | bytes 1048592 | tf_op jit(solution)/shard_map/psum | solution.py:49
  525.4 2.5 fusion.35
  529.8 49.6 %reduce-scatter.13.cloned.1.call-done = bf16[32,256]{1,0:T(8,128)(2,1)} async-done(((bf16[128,256]{1,0:T(8,128)(2,1)}), bf16[32,256]{1,0:T(8,128)(2,1)}) %reduce-scatter.13.cloned.1.call-update) | async-done | bytes 16400 | tf_op jit(solution)/shard_map/reduce_scatter | solution.py:93
  581.5 3.2 collective-permute-done.2
  584.7 15.4 %all_gather.22 = bf16[128,256]{1,0:T(8,128)(2,1)S(1)} all-gather(bf16[32,256]{1,0:T(8,128)(2,1)S(1)} %bitcast_select_fusion), channel_id=1, replica_groups=mesh['section'=16,'row'=4,'col'=8] {'row'}, dimensions={0}, use_global_device_ids=true | all-gather | bytes 81920 | tf_op jit(solution)/shard_map/all_gather | solution.py:80
  601.4 111.2 %all-reduce.11.cloned.1.call-done = bf16[128,2048]{1,0:T(8,128)(2,1)} async-done(((bf16[128,2048]{1,0:T(8,128)(2,1)}), bf16[128,2048]{1,0:T(8,128)(2,1)}) %all-reduce.11.cloned.1.call-update) | async-done | bytes 524304 | tf_op jit(solution)/shard_map/psum | solution.py:85
  712.7 1.6 fusion.27
  715.5 50.1 %reduce-scatter.15.cloned.1.call-done = bf16[32,256]{1,0:T(8,128)(2,1)} async-done(((bf16[128,256]{1,0:T(8,128)(2,1)}), bf16[32,256]{1,0:T(8,128)(2,1)}) %reduce-scatter.15.cloned.1.call-update) | async-done | bytes 16400 | tf_op jit(solution)/shard_map/reduce_scatter | solution.py:93
  768.2 2.0 convolution_convert_fusion.11
  772.2 15.4 %all_gather.23 = bf16[128,256]{1,0:T(8,128)(2,1)S(1)} all-gather(bf16[32,256]{1,0:T(8,128)(2,1)S(1)} %bitcast_select_fusion.1), channel_id=1, replica_groups=mesh['section'=16,'row'=4,'col'=8] {'row'}, dimensions={0}, use_global_device_ids=true | all-gather | bytes 81920 | tf_op jit(solution)/shard_map/all_gather | solution.py:80
  788.9 1.4 maximum_bitcast_fusion
  790.2 22.8 %reduce-scatter.11.cloned.1.call-done = bf16[32,256]{1,0:T(8,128)(2,1)} async-done(((bf16[128,256]{1,0:T(8,128)(2,1)}), bf16[32,256]{1,0:T(8,128)(2,1)}) %reduce-scatter.11.cloned.1.call-update) | async-done | bytes 16400 | tf_op jit(solution)/shard_map/reduce_scatter | solution.py:55
  813.8 1.4 maximum_bitcast_fusion.1
  815.2 2.9 fusion.1
  818.1 107.2 %all-reduce.13.cloned.1.call-done = bf16[128,2048]{1,0:T(8,128)(2,1)} async-done(((bf16[128,2048]{1,0:T(8,128)(2,1)}), bf16[128,2048]{1,0:T(8,128)(2,1)}) %all-reduce.13.cloned.1.call-update) | async-done | bytes 524304 | tf_op jit(solution)/shard_map/psum | solution.py:85
  925.3 1.6 fusion.19
  928.1 2.8 fusion
  930.8 47.1 %reduce-scatter.17.cloned.1.call-done = bf16[32,256]{1,0:T(8,128)(2,1)} async-done(((bf16[128,256]{1,0:T(8,128)(2,1)}), bf16[32,256]{1,0:T(8,128)(2,1)}) %reduce-scatter.17.cloned.1.call-update) | async-done | bytes 16400 | tf_op jit(solution)/shard_map/reduce_scatter | solution.py:93
  978.7 1.3 maximum_bitcast_fusion.2
  (75 shorter events, 27.6 us)
Async XLA Ops:
  7.2 142.5 %copy-start = (bf16[1,2048,256]{2,1,0:T(8,128)(2,1)S(1)}, bf16[1,2048,256]{2,1,0:T(8,128)(2,1)}, u32[]{:S(2)}) copy-start(bf16[1,2048,256]{2,1,0:T(8,128)(2,1)} %param.12) | copy-start | bytes 3145732
  7.2 141.1 %all-reduce.7.cloned.1.call-start = ((), (), s32[]{:S(2)}) async-start(), calls=%async_computation.6 | async-start | bytes 1048576 | tf_op jit(solution)/shard_map/psum | solution.py:49
  31.6 169.8 %reduce-scatter.7.cloned.1.call-start = ((), (), s32[]{:S(2)}) async-start(), calls=%async_computation.7 | async-start | bytes 81920 | tf_op jit(solution)/shard_map/reduce_scatter | solution.py:55
  149.6 1.1 copy-start.11
  149.7 51.8 %copy-start.8 = (bf16[1,3,32,256]{3,2,1,0:T(8,128)(2,1)S(1)}, bf16[1,3,32,256]{3,2,1,0:T(8,128)(2,1)}, u32[]{:S(2)}) copy-start(bf16[1,3,32,256]{3,2,1,0:T(8,128)(2,1)} %param.7) | copy-start | bytes 147460
  149.7 73.8 %copy-start.1 = (bf16[1,256,2048]{2,1,0:T(8,128)(2,1)S(1)}, bf16[1,256,2048]{2,1,0:T(8,128)(2,1)}, u32[]{:S(2)}) copy-start(bf16[1,256,2048]{2,1,0:T(8,128)(2,1)} %param.11) | copy-start | bytes 3145732
  150.6 183.4 %all-reduce.9.cloned.1.call-start = ((), (), s32[]{:S(2)}) async-start(), calls=%async_computation.8 | async-start | bytes 1048576 | tf_op jit(solution)/shard_map/psum | solution.py:49
  202.8 5.2 collective-permute-start
  224.6 162.5 %reduce-scatter.9.cloned.1.call-start = ((), (), s32[]{:S(2)}) async-start(), calls=%async_computation.9 | async-start | bytes 81920 | tf_op jit(solution)/shard_map/reduce_scatter | solution.py:55
  335.4 0.8 copy-start.2
  336.2 1.0 slice-start
  337.1 188.2 %all-reduce.15.cloned.1.call-start = ((), (), s32[]{:S(2)}) async-start(), calls=%async_computation.16 | async-start | bytes 2097152 | tf_op jit(solution)/shard_map/psum | solution.py:49
  388.4 6.5 collective-permute-start.1
  395.6 15.8 %copy-start.4 = (bf16[32,256]{1,0:T(8,128)(2,1)}, bf16[32,256]{1,0:T(8,128)(2,1)S(1)}, u32[]{:S(2)}) copy-start(bf16[32,256]{1,0:T(8,128)(2,1)S(1)} %fusion.67) | copy-start | bytes 49156
  411.4 168.0 %reduce-scatter.13.cloned.1.call-start = ((), (), s32[]{:S(2)}) async-start(), calls=%async_computation.11 | async-start | bytes 81920 | tf_op jit(solution)/shard_map/reduce_scatter | solution.py:93
  527.8 0.8 copy-start.3
  527.8 51.6 %copy-start.7 = (bf16[1,3,32,256]{3,2,1,0:T(8,128)(2,1)S(1)}, bf16[1,3,32,256]{3,2,1,0:T(8,128)(2,1)}, u32[]{:S(2)}) copy-start(bf16[1,3,32,256]{3,2,1,0:T(8,128)(2,1)} %param.13) | copy-start | bytes 147460
  529.8 182.9 %all-reduce.11.cloned.1.call-start = ((), (), s32[]{:S(2)}) async-start(), calls=%async_computation.12 | async-start | bytes 1048576 | tf_op jit(solution)/shard_map/psum | solution.py:85
  580.2 4.5 copy-start.9
  580.2 4.5 collective-permute-start.2
  601.4 164.2 %reduce-scatter.15.cloned.1.call-start = ((), (), s32[]{:S(2)}) async-start(), calls=%async_computation.13 | async-start | bytes 81920 | tf_op jit(solution)/shard_map/reduce_scatter | solution.py:93
  715.4 97.6 %reduce-scatter.11.cloned.1.call-start = ((), (), s32[]{:S(2)}) async-start(), calls=%async_computation.10 | async-start | bytes 81920 | tf_op jit(solution)/shard_map/reduce_scatter | solution.py:55
  766.9 4.7 collective-permute-start.3
  770.2 155.1 %all-reduce.13.cloned.1.call-start = ((), (), s32[]{:S(2)}) async-start(), calls=%async_computation.14 | async-start | bytes 1048576 | tf_op jit(solution)/shard_map/psum | solution.py:85
  771.6 0.6 copy-start.5
  788.8 189.1 %reduce-scatter.17.cloned.1.call-start = ((), (), s32[]{:S(2)}) async-start(), calls=%async_computation.15 | async-start | bytes 81920 | tf_op jit(solution)/shard_map/reduce_scatter | solution.py:93
  928.1 49.8 %copy-start.6 = (bf16[32,256]{1,0:T(8,128)(2,1)S(1)}, bf16[32,256]{1,0:T(8,128)(2,1)}, u32[]{:S(2)}) copy-start(bf16[32,256]{1,0:T(8,128)(2,1)} %copy-done.5) | copy-start | bytes 49156
  928.1 50.6 %copy-start.10 = (bf16[32,256]{1,0:T(8,128)(2,1)S(1)}, bf16[32,256]{1,0:T(8,128)(2,1)}, u32[]{:S(2)}) copy-start(bf16[32,256]{1,0:T(8,128)(2,1)} %copy-done.9) | copy-start | bytes 49156
Sparse Core Ops, SparseCore 0:
  31.8 116.5 all-reduce.6
  152.1 49.3 reduce-scatter.6
  224.7 109.2 all-reduce.8
  337.7 49.3 reduce-scatter.8
  411.5 113.7 all-reduce.14
  529.9 49.5 reduce-scatter.12
  601.5 111.1 all-reduce.10
  716.2 49.3 reduce-scatter.14
  770.3 42.7 reduce-scatter.10
  815.8 109.4 all-reduce.12
  928.5 49.3 reduce-scatter.16
where the time goes:
time: 988 us; the launch traced here: 987 us
  waiting for transfers between devices  811 us (82%)
  blocking collectives  100 us (10%)
  matrix products  21.2 us (2%)
  other arithmetic  20.1 us (2%)
  between operations  19.9 us (2%)
    psum x5, waiting for transfers between devices, per_device(): lax.psum(partial_value.astype(jnp.bfloat16), 'col').astype(jnp.float32)  558 us
    reduce_scatter x3, waiting for transfers between devices, per_device(): lax.psum_scatter(feature_term(jnp.int32(0), piece_rows * lax.axis_size('r...  147 us
    reduce_scatter x3, waiting for transfers between devices, per_device(): lax.psum_scatter(down_term(jnp.int32(0), piece_rows * lax.axis_size('row'...  101 us
    all_gather x3, blocking collectives, per_device(): full_grad = lax.all_gather(grad_out, 'row', axis=0, tiled=True)  50.5 us
    all_gather x3, blocking collectives, per_device(): full_in = lax.all_gather(act_in, 'row', axis=0, tiled=True)  49.9 us
  transfers between devices with their start and end apart: 15, of which 13 were waited for; matrix products, arithmetic and copies ran while one was open for 1% of the time, Pallas kernels for 0%

commit v1 on v0

v1 whole, which is shorter than its diff:
```python
import jax
import jax.numpy as jnp
from jax import lax
from jax.experimental import pallas as pl
from jax.experimental.pallas import tpu as pltpu
from jax.sharding import PartitionSpec as P

MESH = pl.DeviceIdType.MESH
GROUP = 4
F32 = jnp.float32
BF16 = jnp.bfloat16


def sigmoid(value):
    return 1.0 / (1.0 + jnp.exp(-value))


def kernel(
    ids, inputs, send_base, recv_base, w_up, w_down, cotangent,
    sec_in, sec_out, in_grad, grad_up, grad_down,
    xs, gs, stage, base, late, act, gpre, pre, gsum,
    a_out, a_in, b_out, b_in, part, swap_in, p_out, relay_in, own_in,
    pre_send, pre_recv, a_send, a_recv, b_send, b_recv, c_send, c_recv,
    s_send, s_recv, r_send, r_recv, o_send, o_recv,
):
    ticks, rows, width = inputs.shape
    tokens = xs.shape[0] // ticks
    chunks = tokens // rows
    half = rows // 2
    shard = act.shape[2]
    section, row, col = (lax.axis_index(n) for n in ("section", "row", "col"))
    sections, n_row, n_col = (lax.axis_size(n) for n in ("section", "row", "col"))
    core = lax.rem(row, 2)
    place = lax.rem(col, GROUP)
    first = col - place
    mates = [{"col": first + lax.rem(place + d, GROUP)} for d in range(1, GROUP)]
    across = {"col": lax.rem(col + GROUP, n_col)}
    peers = [{"row": lax.rem(row + d, n_row)} for d in range(1, n_row)]
    twin = {"row": row + 1 - 2 * core}
    ahead = lax.rem(section + 1, sections)
    behind = lax.rem(section + sections - 1, sections)
    ahead_ids = [{"section": ahead, "row": lax.rem(row + d, n_row)} for d in range(n_row)]
    behind_ids = [{"section": behind, "row": lax.rem(row + d, n_row)} for d in range(n_row)]

    def remote(src, dst, send_sem, recv_sem, where):
        pltpu.make_async_remote_copy(
            src_ref=src, dst_ref=dst, send_sem=send_sem, recv_sem=recv_sem,
            device_id=where, device_id_type=MESH,
        ).start()

    def await_bytes(ref, sem):
        pltpu.make_async_copy(ref, ref, sem).wait()

    def chunk_rows(tick, chunk):
        return pl.ds(pl.multiple_of(tick * tokens + chunk * rows, rows), rows)

    def own_rows(tick):
        return chunk_rows(tick, row)

    def pick(table, tick):
        return table[ids[tick - section + sections - 1]]

    def each(task):
        def body(chunk, carry):
            task(chunk)
            return carry

        lax.fori_loop(0, chunks, body, 0)

    barrier = pltpu.get_barrier_semaphore()
    friends = mates + [across] + peers + ahead_ids + behind_ids
    for friend in friends:
        pl.semaphore_signal(barrier, inc=1, device_id=friend, device_id_type=MESH)
    pl.semaphore_wait(barrier, len(friends))

    for peer in peers:
        remote(inputs.at[0], xs.at[own_rows(0)], pre_send.at[0], pre_recv.at[0], peer)
    for tick in range(1, ticks):
        stage[tick - 1] = jnp.where(section == 0, inputs[tick], pick(recv_base, tick))
    for peer in peers:
        remote(cotangent.at[ticks - 1], gs.at[own_rows(ticks - 1)], pre_send.at[1], pre_recv.at[1], peer)
    for peer in peers:
        for tick in range(1, ticks):
            remote(stage.at[tick - 1], base.at[tick - 1, pl.ds(row * rows, rows)], pre_send.at[2], pre_recv.at[2], peer)
    last = section == sections - 1

    @pl.when(last)
    def _():
        for peer in peers:
            for tick in range(ticks - 1):
                remote(cotangent.at[tick], late.at[tick, pl.ds(row * rows, rows)], pre_send.at[3], pre_recv.at[3], peer)

    xs[own_rows(0), :] = inputs[0]
    gs[own_rows(ticks - 1), :] = cotangent[ticks - 1]
    for tick in range(1, ticks):
        base[tick - 1, pl.ds(pl.multiple_of(row * rows, rows), rows), :] = stage[tick - 1]
    for tick in range(ticks - 1):
        late[tick, pl.ds(pl.multiple_of(row * rows, rows), rows), :] = cotangent[tick]

    def expand(phase, tick, source, weight):
        def task(chunk):
            value = source[chunk_rows(tick, chunk), :]
            for d in (1, 2, 3, 0):
                columns = pl.ds(pl.multiple_of(lax.rem(place + d, GROUP) * shard, shard), shard)
                a_out[phase, chunk, d] = weight(value, columns).astype(BF16)
                if d:
                    remote(a_out.at[phase, chunk, d], a_in.at[phase, chunk, d - 1], a_send.at[phase], a_recv.at[phase, chunk], mates[d - 1])

        return task

    def up(value, columns):
        return jnp.dot(value, w_up[:, columns], preferred_element_type=F32)

    def down_t(value, columns):
        return lax.dot_general(value, w_down[columns, :], (((1,), (1,)), ((), ())), preferred_element_type=F32)

    def combine(phase):
        def task(chunk):
            await_bytes(a_in.at[phase, chunk], a_recv.at[phase, chunk])
            total = a_out[phase, chunk, 0].astype(F32)
            for d in range(GROUP - 1):
                total = total + a_in[phase, chunk, d].astype(F32)
            b_out[phase, chunk] = total.astype(BF16)
            remote(b_out.at[phase, chunk], b_in.at[phase, chunk], b_send.at[phase], b_recv.at[phase, chunk], across)

        return task

    def summed(phase, chunk):
        await_bytes(b_in.at[phase, chunk], b_recv.at[phase, chunk])
        return b_out[phase, chunk].astype(F32) + b_in[phase, chunk].astype(F32)

    def spread(phase, tick, chunk, hidden):
        for mate in mates:
            ref = hidden.at[place, chunk_rows(tick, chunk)]
            remote(ref, ref, c_send.at[phase], c_recv.at[phase, chunk], mate)

    def activate(phase, tick):
        def task(chunk):
            value = summed(phase, chunk)
            pre[chunk_rows(tick, chunk), :] = value
            act[place, chunk_rows(tick, chunk), :] = (value * sigmoid(value)).astype(BF16)
            spread(phase, tick, chunk, act)

        return task

    def slope(value):
        sig = sigmoid(value)
        return sig * (1.0 + value * (1.0 - sig))

    def differentiate(phase, tick):
        def task(chunk):
            value = summed(phase, chunk) * slope(pre[chunk_rows(tick, chunk), :])
            gpre[place, chunk_rows(tick, chunk), :] = value.astype(BF16)
            spread(phase, tick, chunk, gpre)

        return task

    def contract(phase, tick, hidden, weight, skip):
        def task(chunk):
            await_bytes(hidden.at[pl.ds(0, GROUP - 1), chunk_rows(tick, chunk)], c_recv.at[phase, chunk])
            total = jnp.where(row == chunk, skip(), 0.0)
            for j in range(GROUP):
                total = total + weight(hidden[j, chunk_rows(tick, chunk), :], pl.ds(j * shard, shard))
            part[phase, chunk, 0] = total[:half]
            part[phase, chunk, 1] = total[half:]
            remote(part.at[phase, chunk, 1 - core], swap_in.at[phase, chunk], s_send.at[phase], s_recv.at[phase, chunk], twin)

        return task

    def down(value, columns):
        return jnp.dot(value, w_down[columns, :], preferred_element_type=F32)

    def up_t(value, columns):
        return lax.dot_general(value, w_up[:, columns], (((1,), (1,)), ((), ())), preferred_element_type=F32)

    def forward_skip(tick):
        return lambda: xs[own_rows(tick), :].astype(F32) - pick(send_base, tick).astype(F32)

    def backward_skip(tick):
        return lambda: gs[own_rows(tick), :].astype(F32)

    def hand_on(phase, targets):
        def task(chunk):
            await_bytes(swap_in.at[phase, chunk], s_recv.at[phase, chunk])
            total = part[phase, chunk, core] + swap_in[phase, chunk]
            p_out[phase, chunk] = total.astype(BF16)
            for target in targets:
                remote(p_out.at[phase, chunk], relay_in.at[phase, chunk, row], r_send.at[phase], r_recv.at[phase, chunk], target)

            @pl.when(row == chunk)
            def _():
                own_in[phase, row] = p_out[phase, chunk]

            @pl.when(row != chunk)
            def _():
                remote(p_out.at[phase, chunk], own_in.at[phase, row], o_send.at[phase], o_recv.at[phase], {"row": chunk})

        return task

    def halves(ref):
        low = ref[0].astype(F32) + ref[2].astype(F32)
        high = ref[1].astype(F32) + ref[3].astype(F32)
        return jnp.concatenate([low, high], axis=0)

    def enter(phase, tick):
        def task(chunk):
            await_bytes(relay_in.at[phase, chunk], r_recv.at[phase, chunk])
            here = base[tick - 1, pl.ds(pl.multiple_of(chunk * rows, rows), rows), :]
            rebuilt = (here.astype(F32) + halves(relay_in.at[phase, chunk])).astype(BF16)
            xs[chunk_rows(tick, chunk), :] = jnp.where(section == 0, here, rebuilt)

        return task

    def enter_back(phase, tick):
        def task(chunk):
            await_bytes(relay_in.at[phase, chunk], r_recv.at[phase, chunk])
            here = late[tick, pl.ds(pl.multiple_of(chunk * rows, rows), rows), :]
            arrived = halves(relay_in.at[phase, chunk]).astype(BF16)
            gs[chunk_rows(tick, chunk), :] = jnp.where(last, here, arrived)

        return task

    def both(one, two):
        def task(chunk):
            one(chunk)
            two(chunk)

        return task

    def own_sum(phase):
        await_bytes(own_in.at[phase, pl.ds(0, n_row - 1)], o_recv.at[phase])
        return halves(own_in.at[phase])

    def keep_output(tick):
        sec_in[tick] = xs[own_rows(tick), :]
        sec_out[tick] = (own_sum(tick) + pick(send_base, tick).astype(F32)).astype(BF16)

    def keep_grad(tick):
        in_grad[tick] = own_sum(ticks + tick).astype(BF16)

    top = ticks - 1
    back = ticks + top
    await_bytes(xs.at[pl.ds(0, (n_row - 1) * rows)], pre_recv.at[0])
    for tick in range(ticks):
        step = expand(tick, tick, xs, up)
        if tick:
            step = both(enter(tick - 1, tick), step)
        each(step)
        each(combine(tick))
        if tick < top:
            each(activate(tick, tick))
            each(contract(tick, tick, act, down, forward_skip(tick)))
            each(hand_on(tick, ahead_ids))
        if tick == 0:
            await_bytes(gs.at[pl.ds(0, (n_row - 1) * rows)], pre_recv.at[1])
            await_bytes(base.at[:, pl.ds(0, (n_row - 1) * rows)], pre_recv.at[2])

            @pl.when(last)
            def _():
                await_bytes(late.at[:, pl.ds(0, (n_row - 1) * rows)], pre_recv.at[3])

            each(expand(back, top, gs, down_t))
        if tick == 1:
            each(combine(back))
            keep_output(0)
    each(both(activate(top, top), differentiate(back, top)))
    each(contract(back, top, gpre, up_t, backward_skip(top)))
    each(hand_on(back, behind_ids))
    each(contract(top, top, act, down, forward_skip(top)))
    each(hand_on(top, []))
    keep_output(1)
    for tick in range(top - 1, -1, -1):
        phase = ticks + tick
        each(both(enter_back(phase + 1, tick), expand(phase, tick, gs, down_t)))
        if tick == top - 1:
            keep_output(top)
        each(combine(phase))
        each(differentiate(phase, tick))
        each(contract(phase, tick, gpre, up_t, backward_skip(tick)))
        each(hand_on(phase, behind_ids if tick else []))
        keep_grad(tick + 1)

    contract_first = (((0,), (0,)), ((), ()))
    for j in range(GROUP):
        columns = pl.ds(j * shard, shard)
        grad_up[:, columns] = lax.dot_general(xs[...], gpre[j], contract_first, preferred_element_type=F32).astype(BF16)
        grad_down[columns, :] = lax.dot_general(act[j], gs[...], contract_first, preferred_element_type=F32).astype(BF16)
    keep_grad(0)

    count = (n_row - 1) * rows
    await_bytes(xs.at[pl.ds(0, count)], pre_send.at[0])
    await_bytes(gs.at[pl.ds(0, count)], pre_send.at[1])
    await_bytes(base.at[:, pl.ds(0, count)], pre_send.at[2])

    @pl.when(last)
    def _():
        await_bytes(late.at[:, pl.ds(0, count)], pre_send.at[3])

    for phase in range(2 * ticks):
        await_bytes(a_in.at[phase], a_send.at[phase])
        await_bytes(b_in.at[phase], b_send.at[phase])
        await_bytes(act.at[pl.ds(0, GROUP - 1), pl.ds(0, tokens)], c_send.at[phase])
        await_bytes(swap_in.at[phase], s_send.at[phase])
        if phase != top and phase != ticks:
            await_bytes(relay_in.at[phase], r_send.at[phase])
        await_bytes(own_in.at[phase, pl.ds(0, n_row - 1)], o_send.at[phase])


def per_device(inputs, sample_ids, send_base, recv_base, w_up, w_down, cotangent):
    ticks, rows, width = inputs.shape[1:]
    chunks = lax.axis_size("row")
    tokens = rows * chunks
    hidden = w_up.shape[2]
    shard = hidden // GROUP
    phases = 2 * ticks
    half = rows // 2
    dma = pltpu.SemaphoreType.DMA
    vmem = pl.BlockSpec(memory_space=pltpu.VMEM)
    outs = pl.pallas_call(
        kernel,
        out_shape=[
            jax.ShapeDtypeStruct((ticks, rows, width), BF16),
            jax.ShapeDtypeStruct((ticks, rows, width), BF16),
            jax.ShapeDtypeStruct((ticks, rows, width), BF16),
            jax.ShapeDtypeStruct((width, hidden), BF16),
            jax.ShapeDtypeStruct((hidden, width), BF16),
        ],
        in_specs=[pl.BlockSpec(memory_space=pltpu.SMEM)] + [vmem] * 6,
        out_specs=[vmem] * 5,
        scratch_shapes=[
            pltpu.VMEM((ticks * tokens, width), BF16),
            pltpu.VMEM((ticks * tokens, width), BF16),
            pltpu.VMEM((ticks - 1, rows, width), BF16),
            pltpu.VMEM((ticks - 1, tokens, width), BF16),
            pltpu.VMEM((ticks - 1, tokens, width), BF16),
            pltpu.VMEM((GROUP, ticks * tokens, shard), BF16),
            pltpu.VMEM((GROUP, ticks * tokens, shard), BF16),
            pltpu.VMEM((ticks * tokens, shard), F32),
            pltpu.VMEM((8, 128), F32),
            pltpu.VMEM((phases, chunks, GROUP, rows, shard), BF16),
            pltpu.VMEM((phases, chunks, GROUP - 1, rows, shard), BF16),
            pltpu.VMEM((phases, chunks, rows, shard), BF16),
            pltpu.VMEM((phases, chunks, rows, shard), BF16),
            pltpu.VMEM((phases, chunks, 2, half, width), F32),
            pltpu.VMEM((phases, chunks, half, width), F32),
            pltpu.VMEM((phases, chunks, half, width), BF16),
            pltpu.VMEM((phases, chunks, chunks, half, width), BF16),
            pltpu.VMEM((phases, chunks, half, width), BF16),
            dma((4,)), dma((4,)),
            dma((phases,)), dma((phases, chunks)),
            dma((phases,)), dma((phases, chunks)),
            dma((phases,)), dma((phases, chunks)),
            dma((phases,)), dma((phases, chunks)),
            dma((phases,)), dma((phases, chunks)),
            dma((phases,)), dma((phases,)),
        ],
        compiler_params=pltpu.CompilerParams(
            collective_id=0, has_side_effects=True, vmem_limit_bytes=56 << 20
        ),
    )(sample_ids, inputs[0], send_base[0], recv_base[0], w_up[0], w_down[0], cotangent[0])
    return tuple(value[None] for value in outs)


def solution(mesh):
    pieces = P("section", None, "row", "col")
    ups, downs = P("section", "col", "row"), P("section", "row", "col")
    return jax.shard_map(
        per_device,
        mesh=mesh,
        in_specs=(pieces, P(), pieces, pieces, ups, downs, pieces),
        out_specs=(pieces, pieces, pieces, ups, downs),
        check_vma=False,
    )
```

time: 988 us -> 291 us (0.29)
  the two profiles are of different devices: /device:TPU:1 before, /device:TPU:87 now
where the time goes in v1:
time: 291 us
  Pallas kernels  284 us (98%)
  local copies, waits for them, and re-layouts  6.24 us (2%)
    pallas_call x1, Pallas kernels, per_device(): pl.pallas_call(kernel, out_shape=[jax.ShapeDtypeStruct((ticks, rows, widt...  284 us
    unnamed x11, local copies, waits for them, and re-layouts  6.24 us

profile of v1, /device:TPU:87, one launch (start us, length us, event | category | flops | bytes accessed | tf_op | source)
XLA Modules:
  0.0 291.0 jit_solution(13232835191179772815)
XLA Ops:
  0.6 284.1 %shard_map.110 = (bf16[3,32,256]{2,1,0:T(8,128)(2,1)}, bf16[3,32,256]{2,1,0:T(8,128)(2,1)}, bf16[3,32,256]{2,1,0:T(8,128)(2,1)}, bf16[256,2048]{1,0:T(8,128)(2,1)}, bf16[2048,256]{1,0:T(8,128)(2,1)}) custom-call(s32[18]{0:T(128)} %ids.1, bf16[3,32,256]{2,1,0:T(8,128)(2,1)} %bitcast.20, bf16[16,32,256]{2,1,0:T(8,128)(2,1)} %bitcast.15, ...), custom_call_target="tpu_custom_call" | custom-call | tf_op jit(solution)/shard_map/pallas_call | solution.py:319
  284.7 0.0 copy-start.2
  284.7 1.4 copy.17
  286.2 0.0 copy-done.2
  286.2 0.0 copy-start.1
  286.2 0.6 copy.18
  286.8 0.2 copy-done.1
  287.0 0.6 copy.19
  287.6 0.0 copy-start
  287.6 2.4 copy.20
  290.0 0.0 copy-done
  290.0 1.0 copy.21
Async XLA Ops:
  284.7 1.4 copy-start.2
  286.2 0.8 copy-start.1
  287.6 2.4 copy-start

commit v2 on v1

v2 whole, which is shorter than its diff:
```python
import jax
import jax.numpy as jnp
from jax import lax
from jax.experimental import pallas as pl
from jax.experimental.pallas import tpu as pltpu
from jax.sharding import PartitionSpec as P

MESH = pl.DeviceIdType.MESH
GROUP = 4
SIZE = 16
PERIOD = 34
STRIDE = 3
AT_COMBINE, AT_GATHER, AT_ACTIVATE, AT_FORWARD, AT_CONTRACT, AT_HAND = 4, 9, 14, 19, 25, 26
EARLY_START, EARLY_EVERY = 19, 3
SPARE_START, SPARE_EVERY = 106, 3
F32 = jnp.float32
BF16 = jnp.bfloat16


def kernel(
    ids, inputs, send_base, recv_base, w_up, w_down, cotangent,
    sec_in, sec_out, in_grad, grad_up, grad_down,
    up_t, down_t, xs, gs, stage, base, late, act, gpre, pre,
    a_out, a_in, c_out, b_out, b_in, part, swap_in, p_out, relay_in, own_in,
    pre_send, pre_recv, a_send, a_recv, b_send, b_recv, c_send, c_recv,
    s_send, s_recv, r_send, r_recv, o_send, o_recv,
):
    ticks, rows, width = inputs.shape
    tokens = xs.shape[0] // ticks
    chunks, size, wide = a_out.shape[1], a_out.shape[3], a_out.shape[4]
    per_row = rows // size
    half = width // 2
    top = ticks - 1
    phases = 2 * ticks
    section, row, col = (lax.axis_index(n) for n in ("section", "row", "col"))
    sections, n_row, n_col = (lax.axis_size(n) for n in ("section", "row", "col"))
    core = lax.rem(row, 2)
    place = lax.rem(col, GROUP)
    first = col - place
    rank = jnp.where(first == 0, GROUP - 1 - place, place)

    def at_rank(number):
        return {"col": first + jnp.where(first == 0, GROUP - 1 - number, number)}

    mates = [{"col": first + lax.rem(place + d, GROUP)} for d in range(1, GROUP)]
    across = {"col": n_col - 1 - col}
    peers = [{"row": lax.rem(row + d, n_row)} for d in range(1, n_row)]
    twin = {"row": row + 1 - 2 * core}
    ahead = lax.rem(section + 1, sections)
    behind = lax.rem(section + sections - 1, sections)
    ahead_ids = [{"section": ahead, "row": lax.rem(row + d, n_row)} for d in range(n_row)]
    behind_ids = [{"section": behind, "row": lax.rem(row + d, n_row)} for d in range(n_row)]

    def remote(src, dst, send_sem, recv_sem, where):
        pltpu.make_async_remote_copy(
            src_ref=src, dst_ref=dst, send_sem=send_sem, recv_sem=recv_sem,
            device_id=where, device_id_type=MESH,
        ).start()

    def await_bytes(ref, sem):
        pltpu.make_async_copy(ref, ref, sem).wait()

    def span(start, count):
        return pl.ds(pl.multiple_of(start, count), count)

    def chunk_rows(tick, chunk):
        return span(tick * tokens + chunk * size, size)

    def own_rows(tick):
        return span(tick * tokens + row * rows, rows)

    def pick(table, tick):
        return table[ids[tick - section + sections - 1]]

    barrier = pltpu.get_barrier_semaphore()
    friends = mates + [across] + peers + ahead_ids + behind_ids
    for friend in friends:
        pl.semaphore_signal(barrier, inc=1, device_id=friend, device_id_type=MESH)
    pl.semaphore_wait(barrier, len(friends))

    last = section == sections - 1
    for peer in peers:
        remote(inputs.at[0], xs.at[own_rows(0)], pre_send.at[0], pre_recv.at[0], peer)
    for tick in range(1, ticks):
        stage[tick - 1] = jnp.where(section == 0, inputs[tick], pick(recv_base, tick))
    for peer in peers:
        remote(cotangent.at[top], gs.at[own_rows(top)], pre_send.at[1], pre_recv.at[1], peer)
    for peer in peers:
        for tick in range(1, ticks):
            remote(stage.at[tick - 1], base.at[tick - 1, span(row * rows, rows)], pre_send.at[2], pre_recv.at[2], peer)

    @pl.when(last)
    def _():
        for peer in peers:
            for tick in range(top):
                remote(cotangent.at[tick], late.at[tick, span(row * rows, rows)], pre_send.at[3], pre_recv.at[3], peer)

    xs[own_rows(0), :] = inputs[0]
    gs[own_rows(top), :] = cotangent[top]
    for tick in range(1, ticks):
        base[tick - 1, span(row * rows, rows), :] = stage[tick - 1]
    for tick in range(top):
        late[tick, span(row * rows, rows), :] = cotangent[tick]

    early_half = jnp.where(rank >= 2, 1, 0)
    early_to = at_rank(jnp.where(rank == 1, 0, 1))
    early_slot = jnp.where(rank == 3, 0, 1)

    def expand(phase, chunk, value, product):
        def compute(side):
            a_out[phase, chunk, side] = product(value, span(side * wide, wide)).astype(BF16)

        compute(early_half)

        @pl.when(rank > 0)
        def _():
            remote(a_out.at[phase, chunk, early_half], a_in.at[phase, chunk, early_slot], a_send.at[phase], a_recv.at[phase, chunk], early_to)

        compute(1 - early_half)

        @pl.when(rank == 3)
        def _():
            remote(a_out.at[phase, chunk, 0], a_in.at[phase, chunk, 0], a_send.at[phase], a_recv.at[phase, chunk], at_rank(2))

    def expand_forward(tick, chunk):
        def product(value, columns):
            return jnp.dot(value, w_up[:, columns], preferred_element_type=F32)

        expand(tick, chunk, xs[chunk_rows(tick, chunk), :], product)

    def expand_back(tick, chunk):
        def product(value, columns):
            return jnp.dot(value, down_t[:, columns], preferred_element_type=F32)

        expand(ticks + tick, chunk, gs[chunk_rows(tick, chunk), :], product)

    def partial_sum(phase, chunk, side, slots):
        total = a_out[phase, chunk, side].astype(F32)
        for slot in slots:
            total = total + a_in[phase, chunk, slot].astype(F32)
        return total.astype(BF16)

    def combine(phase, chunk):
        def pass_on(side, slots, slot):
            await_bytes(a_in.at[phase, chunk, pl.ds(0, slots)], a_recv.at[phase, chunk])
            c_out[phase, chunk] = partial_sum(phase, chunk, side, range(slots))
            remote(c_out.at[phase, chunk], a_in.at[phase, chunk, slot], a_send.at[phase], a_recv.at[phase, chunk], at_rank(0))

        @pl.when(rank == 2)
        def _():
            pass_on(0, 1, 0)

        @pl.when(rank == 1)
        def _():
            pass_on(1, 2, 2)

    def gather(phase, chunk):
        await_bytes(a_in.at[phase, chunk], a_recv.at[phase, chunk])
        b_out[phase, chunk, 0] = partial_sum(phase, chunk, 0, (0, 1))
        b_out[phase, chunk, 1] = partial_sum(phase, chunk, 1, (2,))
        remote(b_out.at[phase, chunk], b_in.at[phase, chunk], b_send.at[phase], b_recv.at[phase, chunk], across)

    def summed(phase, chunk):
        await_bytes(b_in.at[phase, chunk], b_recv.at[phase, chunk])
        return b_out[phase, chunk].astype(F32) + b_in[phase, chunk].astype(F32)

    def spread(phase, tick, chunk, hidden):
        def send(side, number):
            ref = hidden.at[side, chunk_rows(tick, chunk)]
            remote(ref, ref, c_send.at[phase], c_recv.at[phase, chunk, side], at_rank(number))

        send(1, 1)
        send(0, 2)
        send(0, 1)

    def forward(phase, tick, chunk, hidden):
        def pass_on(side, numbers):
            ref = hidden.at[side, chunk_rows(tick, chunk)]
            await_bytes(ref, c_recv.at[phase, chunk, side])
            for number in numbers:
                remote(ref, ref, c_send.at[phase], c_recv.at[phase, chunk, side], at_rank(number))

        @pl.when(rank == 1)
        def _():
            pass_on(1, (3, 2))

        @pl.when(rank == 2)
        def _():
            pass_on(0, (3,))

    def activate(tick, chunk):
        value = summed(tick, chunk)
        pre[:, chunk_rows(tick, chunk), :] = value
        act[:, chunk_rows(tick, chunk), :] = (value / (1.0 + jnp.exp(-value))).astype(BF16)

    def differentiate(tick, chunk):
        value = pre[:, chunk_rows(tick, chunk), :]
        sig = 1.0 / (1.0 + jnp.exp(-value))
        slope = sig * (1.0 + value * (1.0 - sig))
        gpre[:, chunk_rows(tick, chunk), :] = (summed(ticks + tick, chunk) * slope).astype(BF16)
        spread(ticks + tick, tick, chunk, gpre)

    def await_hidden(phase, tick, chunk, hidden):
        for side, known in ((0, 2), (1, 1)):
            @pl.when(jnp.logical_and(rank != 0, rank != known))
            def _(side=side):
                await_bytes(hidden.at[side, chunk_rows(tick, chunk)], c_recv.at[phase, chunk, side])

    def swap(phase, chunk, total, skip):
        def halves(value):
            return value[:, :half], value[:, half:]

        part[phase, chunk, 0], part[phase, chunk, 1] = halves(total)

        @pl.when(row == lax.div(chunk, per_row))
        def _():
            part[phase, chunk, 0], part[phase, chunk, 1] = halves(total + skip())

        remote(part.at[phase, chunk, 1 - core], swap_in.at[phase, chunk], s_send.at[phase], s_recv.at[phase, chunk], twin)

    def contract_forward(tick, chunk):
        await_hidden(tick, tick, chunk, act)
        total = 0.0
        for side in range(2):
            total = total + jnp.dot(act[side, chunk_rows(tick, chunk), :], w_down[pl.ds(side * wide, wide), :], preferred_element_type=F32)

        def skip():
            sample = ids[tick - section + sections - 1]
            stored = send_base[sample, span(lax.rem(chunk, per_row) * size, size), :]
            return xs[chunk_rows(tick, chunk), :].astype(F32) - stored.astype(F32)

        swap(tick, chunk, total, skip)

    def contract_back(tick, chunk):
        await_hidden(ticks + tick, tick, chunk, gpre)
        total = 0.0
        for side in range(2):
            total = total + jnp.dot(gpre[side, chunk_rows(tick, chunk), :], up_t[pl.ds(side * wide, wide), :], preferred_element_type=F32)
        swap(ticks + tick, chunk, total, lambda: gs[chunk_rows(tick, chunk), :].astype(F32))

    def hand_on(phase, chunk):
        await_bytes(swap_in.at[phase, chunk], s_recv.at[phase, chunk])
        p_out[phase, chunk] = (part[phase, chunk, core] + swap_in[phase, chunk]).astype(BF16)

        def relay(targets):
            for target in targets:
                remote(p_out.at[phase, chunk], relay_in.at[phase, chunk, row], r_send.at[phase], r_recv.at[phase, chunk], target)

        @pl.when(phase < top)
        def _():
            relay(ahead_ids)

        @pl.when(phase > ticks)
        def _():
            relay(behind_ids)

        @pl.when(lax.rem(chunk, per_row) == per_row - 1)
        def _():
            holder = lax.div(chunk, per_row)
            ready = p_out.at[phase, pl.ds(holder * per_row, per_row)]

            @pl.when(row == holder)
            def _():
                own_in[phase, row] = ready[...]

            @pl.when(row != holder)
            def _():
                remote(ready, own_in.at[phase, row], o_send.at[phase], o_recv.at[phase], {"row": holder})

    def joined(ref):
        low = ref[0].astype(F32) + ref[2].astype(F32)
        high = ref[1].astype(F32) + ref[3].astype(F32)
        return jnp.concatenate([low, high], axis=1)

    def enter_forward(tick, chunk):
        phase = tick - 1
        await_bytes(relay_in.at[phase, chunk], r_recv.at[phase, chunk])
        here = base[tick - 1, span(chunk * size, size), :]
        rebuilt = (here.astype(F32) + joined(relay_in.at[phase, chunk])).astype(BF16)
        xs[chunk_rows(tick, chunk), :] = jnp.where(section == 0, here, rebuilt)

    def enter_back(tick, chunk):
        phase = ticks + tick + 1
        await_bytes(relay_in.at[phase, chunk], r_recv.at[phase, chunk])
        here = late[tick, span(chunk * size, size), :]
        arrived = joined(relay_in.at[phase, chunk]).astype(BF16)
        gs[chunk_rows(tick, chunk), :] = jnp.where(last, here, arrived)

    def own_sum(phase):
        await_bytes(own_in.at[phase, pl.ds(0, n_row - 1)], o_recv.at[phase])
        return jnp.concatenate([joined(own_in.at[phase, :, piece]) for piece in range(per_row)], axis=0)

    def turn_weights(block, carry):
        hidden_block = span(block * width, width)
        up_t[hidden_block, :] = w_up[:, hidden_block].T
        down_t[:, hidden_block] = w_down[hidden_block, :].T
        return carry

    lax.fori_loop(0, w_up.shape[1] // width, turn_weights, 0)
    await_bytes(xs.at[pl.ds(0, (n_row - 1) * rows)], pre_recv.at[0])
    rounds = 2 * ticks - 1

    def when(condition):
        return pl.when(condition)

    def place_of(step, offset):
        time = step - offset
        turn = lax.div(time, PERIOD)
        inside = lax.rem(time, PERIOD)
        chunk = lax.div(inside, STRIDE)
        due = jnp.logical_and(chunk < chunks, lax.rem(inside, STRIDE) == 0)
        valid = jnp.logical_and(time >= 0, jnp.logical_and(due, turn < rounds))
        return turn, jnp.minimum(chunk, chunks - 1), valid

    def side_of(step, offset, every):
        time = step - offset
        chunk = lax.div(time, every)
        due = jnp.logical_and(time >= 0, jnp.logical_and(chunk < chunks, lax.rem(time, every) == 0))
        return jnp.minimum(chunk, chunks - 1), due

    back_top = ticks + top

    def phase_of(turn, switch):
        return jnp.where(turn < switch, turn, ticks + 2 * top - turn)

    def body(step, carry):
        turn, chunk, valid = place_of(step, AT_HAND)
        spare, spare_due = side_of(step, SPARE_START + AT_HAND - AT_ACTIVATE, SPARE_EVERY)

        @when(valid)
        def _():
            hand_on(phase_of(turn, top), chunk)

        @when(spare_due)
        def _():
            hand_on(top, spare)

        turn, chunk, valid = place_of(step, AT_CONTRACT)
        spare, spare_due = side_of(step, SPARE_START + AT_CONTRACT - AT_ACTIVATE, SPARE_EVERY)

        @when(jnp.logical_and(valid, turn < top))
        def _():
            contract_forward(turn, chunk)

        @when(jnp.logical_and(valid, turn >= top))
        def _():
            contract_back(2 * top - turn, chunk)

        @when(spare_due)
        def _():
            contract_forward(top, spare)

        @when(jnp.logical_or(rank == 1, rank == 2))
        def _():
            turn, chunk, valid = place_of(step, AT_FORWARD)
            spare, spare_due = side_of(step, SPARE_START + AT_FORWARD - AT_ACTIVATE, SPARE_EVERY)

            @when(jnp.logical_and(valid, turn < top))
            def _():
                forward(turn, turn, chunk, act)

            @when(jnp.logical_and(valid, turn >= top))
            def _():
                forward(ticks + 2 * top - turn, 2 * top - turn, chunk, gpre)

            @when(spare_due)
            def _():
                forward(top, top, spare, act)

            turn, chunk, valid = place_of(step, AT_COMBINE)
            early, early_due = side_of(step, EARLY_START + AT_COMBINE, EARLY_EVERY)

            @when(valid)
            def _():
                combine(phase_of(turn, ticks), chunk)

            @when(early_due)
            def _():
                combine(back_top, early)

        @when(rank == 0)
        def _():
            turn, chunk, valid = place_of(step, AT_ACTIVATE)
            spare, spare_due = side_of(step, SPARE_START, SPARE_EVERY)

            @when(jnp.logical_and(valid, turn <= top))
            def _():
                activate(turn, chunk)

            @when(jnp.logical_and(valid, turn < top))
            def _():
                spread(turn, turn, chunk, act)

            @when(jnp.logical_and(valid, turn >= top))
            def _():
                differentiate(2 * top - turn, chunk)

            @when(spare_due)
            def _():
                spread(top, top, spare, act)

            turn, chunk, valid = place_of(step, AT_GATHER)
            early, early_due = side_of(step, EARLY_START + AT_GATHER, EARLY_EVERY)

            @when(valid)
            def _():
                gather(phase_of(turn, ticks), chunk)

            @when(early_due)
            def _():
                gather(back_top, early)

        e_turn, e_chunk, e_valid = place_of(step, 0)
        early, early_due = side_of(step, EARLY_START, EARLY_EVERY)

        @when(jnp.logical_and(e_valid, e_turn <= top))
        def _():
            @when(e_turn > 0)
            def _():
                enter_forward(e_turn, e_chunk)

            expand_forward(e_turn, e_chunk)

        @when(jnp.logical_and(e_valid, e_turn > top))
        def _():
            enter_back(2 * top - e_turn, e_chunk)
            expand_back(2 * top - e_turn, e_chunk)

        @when(early_due)
        def _():
            expand_back(top, early)

        @when(step == EARLY_START - 1)
        def _():
            await_bytes(gs.at[pl.ds(0, (n_row - 1) * rows)], pre_recv.at[1])
            await_bytes(base.at[:, pl.ds(0, (n_row - 1) * rows)], pre_recv.at[2])

            @when(last)
            def _():
                await_bytes(late.at[:, pl.ds(0, (n_row - 1) * rows)], pre_recv.at[3])

        return carry

    lax.fori_loop(0, (rounds - 1) * PERIOD + chunks * STRIDE + AT_HAND, body, 0)

    contract_first = (((0,), (0,)), ((), ()))
    for side in range(2):
        columns = pl.ds(side * wide, wide)
        grad_up[:, columns] = lax.dot_general(xs[...], gpre[side], contract_first, preferred_element_type=F32).astype(BF16)
        grad_down[columns, :] = lax.dot_general(act[side], gs[...], contract_first, preferred_element_type=F32).astype(BF16)
    for tick in range(ticks):
        sec_in[tick] = xs[own_rows(tick), :]
        sec_out[tick] = (own_sum(tick) + pick(send_base, tick).astype(F32)).astype(BF16)
    for tick in range(top, -1, -1):
        in_grad[tick] = own_sum(ticks + tick).astype(BF16)

    count = (n_row - 1) * rows
    await_bytes(xs.at[pl.ds(0, count)], pre_send.at[0])
    await_bytes(gs.at[pl.ds(0, count)], pre_send.at[1])
    await_bytes(base.at[:, pl.ds(0, count)], pre_send.at[2])

    @pl.when(last)
    def _():
        await_bytes(late.at[:, pl.ds(0, count)], pre_send.at[3])

    for phase in range(phases):
        @pl.when(rank == 0)
        def _(phase=phase):
            await_bytes(b_in.at[phase], b_send.at[phase])
            await_bytes(a_in.at[phase], c_send.at[phase])

        @pl.when(rank > 0)
        def _(phase=phase):
            await_bytes(a_out.at[phase], a_send.at[phase])

        @pl.when(rank == 1)
        def _(phase=phase):
            await_bytes(a_out.at[phase], c_send.at[phase])

        @pl.when(rank == 2)
        def _(phase=phase):
            await_bytes(c_out.at[phase], c_send.at[phase])

        await_bytes(swap_in.at[phase], s_send.at[phase])
        if phase != top and phase != ticks:
            await_bytes(relay_in.at[phase], r_send.at[phase])
        await_bytes(own_in.at[phase, pl.ds(0, n_row - 1)], o_send.at[phase])


def per_device(inputs, sample_ids, send_base, recv_base, w_up, w_down, cotangent):
    ticks, rows, width = inputs.shape[1:]
    n_row = lax.axis_size("row")
    tokens = rows * n_row
    chunks = tokens // SIZE
    hidden = w_up.shape[2]
    wide = hidden // 2
    phases = 2 * ticks
    half = width // 2
    dma = pltpu.SemaphoreType.DMA
    vmem = pl.BlockSpec(memory_space=pltpu.VMEM)
    outs = pl.pallas_call(
        kernel,
        out_shape=[
            jax.ShapeDtypeStruct((ticks, rows, width), BF16),
            jax.ShapeDtypeStruct((ticks, rows, width), BF16),
            jax.ShapeDtypeStruct((ticks, rows, width), BF16),
            jax.ShapeDtypeStruct((width, hidden), BF16),
            jax.ShapeDtypeStruct((hidden, width), BF16),
        ],
        in_specs=[pl.BlockSpec(memory_space=pltpu.SMEM)] + [vmem] * 6,
        out_specs=[vmem] * 5,
        scratch_shapes=[
            pltpu.VMEM((hidden, width), BF16),
            pltpu.VMEM((width, hidden), BF16),
            pltpu.VMEM((ticks * tokens, width), BF16),
            pltpu.VMEM((ticks * tokens, width), BF16),
            pltpu.VMEM((ticks - 1, rows, width), BF16),
            pltpu.VMEM((ticks - 1, tokens, width), BF16),
            pltpu.VMEM((ticks - 1, tokens, width), BF16),
            pltpu.VMEM((2, ticks * tokens, wide), BF16),
            pltpu.VMEM((2, ticks * tokens, wide), BF16),
            pltpu.VMEM((2, ticks * tokens, wide), F32),
            pltpu.VMEM((phases, chunks, 2, SIZE, wide), BF16),
            pltpu.VMEM((phases, chunks, 3, SIZE, wide), BF16),
            pltpu.VMEM((phases, chunks, SIZE, wide), BF16),
            pltpu.VMEM((phases, chunks, 2, SIZE, wide), BF16),
            pltpu.VMEM((phases, chunks, 2, SIZE, wide), BF16),
            pltpu.VMEM((phases, chunks, 2, SIZE, half), F32),
            pltpu.VMEM((phases, chunks, SIZE, half), F32),
            pltpu.VMEM((phases, chunks, SIZE, half), BF16),
            pltpu.VMEM((phases, chunks, n_row, SIZE, half), BF16),
            pltpu.VMEM((phases, n_row, rows // SIZE, SIZE, half), BF16),
            dma((4,)), dma((4,)),
            dma((phases,)), dma((phases, chunks)),
            dma((phases,)), dma((phases, chunks)),
            dma((phases,)), dma((phases, chunks, 2)),
            dma((phases,)), dma((phases, chunks)),
            dma((phases,)), dma((phases, chunks)),
            dma((phases,)), dma((phases,)),
        ],
        compiler_params=pltpu.CompilerParams(
            collective_id=0, has_side_effects=True, vmem_limit_bytes=56 << 20
        ),
    )(sample_ids, inputs[0], send_base[0], recv_base[0], w_up[0], w_down[0], cotangent[0])
    return tuple(value[None] for value in outs)


def solution(mesh):
    pieces = P("section", None, "row", "col")
    ups, downs = P("section", "col", "row"), P("section", "row", "col")
    return jax.shard_map(
        per_device,
        mesh=mesh,
        in_specs=(pieces, P(), pieces, pieces, ups, downs, pieces),
        out_specs=(pieces, pieces, pieces, ups, downs),
        check_vma=False,
    )
```

time: 291 us -> 239 us (0.82)
  the two profiles are of different devices: /device:TPU:87 before, /device:TPU:1 now
where the time goes in v2:
time: 239 us; the launch traced here: 238 us
  Pallas kernels  231 us (97%)
  local copies, waits for them, and re-layouts  6.24 us (3%)
    pallas_call x1, Pallas kernels, per_device(): pl.pallas_call(kernel, out_shape=[jax.ShapeDtypeStruct((ticks, rows, widt...  231 us
    unnamed x11, local copies, waits for them, and re-layouts  6.24 us

profile of v2, /device:TPU:1, one launch (start us, length us, event | category | flops | bytes accessed | tf_op | source)
XLA Modules:
  0.0 238.3 jit_solution(16002388364340169187)
XLA Ops:
  0.6 231.4 %shard_map.110 = (bf16[3,32,256]{2,1,0:T(8,128)(2,1)}, bf16[3,32,256]{2,1,0:T(8,128)(2,1)}, bf16[3,32,256]{2,1,0:T(8,128)(2,1)}, bf16[256,2048]{1,0:T(8,128)(2,1)}, bf16[2048,256]{1,0:T(8,128)(2,1)}) custom-call(s32[18]{0:T(128)} %ids.1, bf16[3,32,256]{2,1,0:T(8,128)(2,1)} %bitcast.20, bf16[16,32,256]{2,1,0:T(8,128)(2,1)} %bitcast.15, ...), custom_call_target="tpu_custom_call" | custom-call | tf_op jit(solution)/shard_map/pallas_call | solution.py:501
  232.0 0.0 copy-start.2
  232.0 1.4 copy.17
  233.4 0.0 copy-done.2
  233.4 0.0 copy-start.1
  233.4 0.6 copy.18
  234.1 0.2 copy-done.1
  234.3 0.6 copy.19
  234.9 0.0 copy-start
  234.9 2.4 %copy.20 = bf16[1,256,2048]{2,1,0:T(8,128)(2,1)} copy(bf16[1,256,2048]{2,1,0:T(8,128)(2,1)} %bitcast.14) | data formatting | bytes 2097152
  237.3 0.0 copy-done
  237.3 1.0 copy.21
Async XLA Ops:
  232.0 1.4 copy-start.2
  233.4 0.8 copy-start.1
  234.9 2.4 %copy-start = (bf16[2048,256]{1,0:T(8,128)(2,1)S(1)}, bf16[2048,256]{1,0:T(8,128)(2,1)}, u32[]{:S(2)}) copy-start(bf16[2048,256]{1,0:T(8,128)(2,1)} %get-tuple-element.14) | copy-start | bytes 3145732

commit v3 on v2

--- a/solution.py
+++ b/solution.py
@@ -10,9 +10,9 @@
 SIZE = 16
 PERIOD = 34
 STRIDE = 3
-AT_COMBINE, AT_GATHER, AT_ACTIVATE, AT_FORWARD, AT_CONTRACT, AT_HAND = 4, 9, 14, 19, 25, 26
+AT_COMBINE, AT_GATHER, AT_ACTIVATE, AT_FORWARD, AT_CONTRACT, AT_HAND = 4, 8, 13, 18, 24, 25
 EARLY_START, EARLY_EVERY = 19, 3
-SPARE_START, SPARE_EVERY = 106, 3
+SPARE_START, SPARE_EVERY = 105, 6
 F32 = jnp.float32
 BF16 = jnp.bfloat16
 
@@ -243,7 +243,7 @@
         p_out[phase, chunk] = (part[phase, chunk, core] + swap_in[phase, chunk]).astype(BF16)
 
         def relay(targets):
-            for target in targets:
+            for target in targets[2:] + targets[:2]:
                 remote(p_out.at[phase, chunk], relay_in.at[phase, chunk, row], r_send.at[phase], r_recv.at[phase, chunk], target)
 
         @pl.when(phase < top)

time: 239 us -> 234 us (0.979)
  Pallas kernels: 231 us -> 227 us
    pallas_call x1, Pallas kernels: 231 us -> 227 us  [per_device(): pl.pallas_call(kernel, out_shape=[jax.ShapeDtypeStruct((ticks, rows, widt...]
where the time goes in v3:
time: 234 us
  Pallas kernels  227 us (97%)
  local copies, waits for them, and re-layouts  6.24 us (3%)
    pallas_call x1, Pallas kernels, per_device(): pl.pallas_call(kernel, out_shape=[jax.ShapeDtypeStruct((ticks, rows, widt...  227 us
    unnamed x11, local copies, waits for them, and re-layouts  6.24 us

profile of v3, /device:TPU:1, one launch (start us, length us, event | category | flops | bytes accessed | tf_op | source)
XLA Modules:
  0.0 233.9 jit_solution(13608196086280658913)
XLA Ops:
  0.6 227.0 %shard_map.110 = (bf16[3,32,256]{2,1,0:T(8,128)(2,1)}, bf16[3,32,256]{2,1,0:T(8,128)(2,1)}, bf16[3,32,256]{2,1,0:T(8,128)(2,1)}, bf16[256,2048]{1,0:T(8,128)(2,1)}, bf16[2048,256]{1,0:T(8,128)(2,1)}) custom-call(s32[18]{0:T(128)} %ids.1, bf16[3,32,256]{2,1,0:T(8,128)(2,1)} %bitcast.20, bf16[16,32,256]{2,1,0:T(8,128)(2,1)} %bitcast.15, ...), custom_call_target="tpu_custom_call" | custom-call | tf_op jit(solution)/shard_map/pallas_call | solution.py:501
  227.6 0.0 copy-start.2
  227.6 1.4 copy.17
  229.0 0.0 copy-done.2
  229.1 0.0 copy-start.1
  229.1 0.6 copy.18
  229.7 0.2 copy-done.1
  229.9 0.6 copy.19
  230.5 0.0 copy-start
  230.5 2.4 %copy.20 = bf16[1,256,2048]{2,1,0:T(8,128)(2,1)} copy(bf16[1,256,2048]{2,1,0:T(8,128)(2,1)} %bitcast.14) | data formatting | bytes 2097152
  232.9 0.0 copy-done
  232.9 1.0 copy.21
Async XLA Ops:
  227.6 1.4 copy-start.2
  229.1 0.8 copy-start.1
  230.5 2.4 %copy-start = (bf16[2048,256]{1,0:T(8,128)(2,1)S(1)}, bf16[2048,256]{1,0:T(8,128)(2,1)}, u32[]{:S(2)}) copy-start(bf16[2048,256]{1,0:T(8,128)(2,1)} %get-tuple-element.14) | copy-start | bytes 3145732
